TPU v7x, 256 devices: a whole 4x4x8 slice. The times are simulated.
256 devices in a mesh: site: 16 (over y_hi, z), bond: 16 (over x, y_lo, core).
Axes of the slice: x: 4, y: 4 (y_hi: 2, y_lo: 2; y = y_hi * 2 + y_lo), z: 8, core: 2. Of those that a mesh axis runs over, the one named last changes fastest.
Arguments:
- mps: bfloat16 [16, 512, 8, 512], P('site', 'bond'), may hold values from -18 to 18
- projection: bfloat16 [16, 4096, 512], P('site'), may hold values from -1.1 to 1.1
- gates: float32 [16, 64, 64], replicated, may hold values from -1.2 to 1.2
Outputs:
- new_mps: bfloat16 [16, 512, 8, 512], P('site', 'bond')
- pair_log_norm: float32 [16], P('site')
All inputs are finite; a program needn't handle non-finite values.
Results may differ from a plain program's by a relative error of at most 0.025.
Values may be sent and summed in bfloat16 or wider, within the bound.
A program may use at most 64 MiB of HBM per device.

v0:
```python
import functools
import math

import jax
import jax.numpy as jnp
from jax import lax
from jax.experimental import pallas as pl
from jax.experimental.pallas import tpu as pltpu
from jax.sharding import PartitionSpec as P

PHYS = 8
CHI = 512
epsilon = 1e-06
MESH = pl.DeviceIdType.MESH
HI = lax.Precision.HIGHEST
F32 = jnp.float32
BF16 = jnp.bfloat16
VMEM = pl.BlockSpec(memory_space=pltpu.VMEM)
ANY = pl.BlockSpec(memory_space=pl.ANY)
VLIM = 56 << 20


def params(cid=None):
    if cid is None:
        return pltpu.CompilerParams(vmem_limit_bytes=VLIM)
    return pltpu.CompilerParams(
        collective_id=cid, has_side_effects=True, vmem_limit_bytes=VLIM
    )


def place():
    s = lax.axis_index("site")
    b = lax.axis_index("bond")
    return s, b // 4, (b // 2) % 2, b % 2


def bond(x, y, c):
    return (x * 2 + y) * 2 + c


def greet(sends_to_me, count):
    barrier = pltpu.get_barrier_semaphore()
    for dev in sends_to_me:
        pl.semaphore_signal(barrier, inc=1, device_id=dev, device_id_type=MESH)
    pl.semaphore_wait(barrier, count)


def rcopy(src, dst, ssem, rsem, dev):
    return pltpu.make_async_remote_copy(
        src_ref=src, dst_ref=dst, send_sem=ssem, recv_sem=rsem,
        device_id=dev, device_id_type=MESH,
    )


class Ring:
    def __init__(self, out, sems, s, x, y, c, h):
        self.out, self.c = out, c
        self.ys, self.yr, self.xs, self.xr, self.cs, self.cr = sems
        self.x, self.h = x, h
        self.xp, self.xm, self.x2 = (x + 1) % 4, (x + 3) % 4, (x + 2) % 4
        self.hn = 1 - h
        self.y_dev = (s, bond(x, 1 - y, c))
        self.xp_dev = (s, bond(self.xp, y, c))
        self.xm_dev = (s, bond(self.xm, y, c))
        self.c_dev = (s, bond(x, y, 1 - c))
        self.partners = [self.y_dev, self.xp_dev, self.xm_dev, self.c_dev]
        self.started, self.core, self.ysend = [], [], []

    def slot(self, xx, yy, k):
        return self.out.at[self.c * 8 + xx * 2 + yy, pl.ds(128 * k, 128)]

    def send(self, ref, ss, rs, dev):
        d = rcopy(ref, ref, ss, rs, dev)
        d.start()
        self.started.append(d)
        return d

    def to_core(self, xx, yy, k):
        i = len(self.core)
        ref = self.slot(xx, yy, k)
        self.core.append(self.send(ref, self.cs.at[i], self.cr.at[i], self.c_dev))

    def home(self, k):
        ref = self.slot(self.x, self.h, k)
        self.ysend.append(self.send(ref, self.ys.at[k], self.yr.at[k], self.y_dev))
        for i, dev in enumerate((self.xp_dev, self.xm_dev)):
            self.send(ref, self.xs.at[i, 0, k], self.xr.at[i, 0, k], dev)
        self.to_core(self.x, self.h, k)

    def arrived(self, i, j, k, xx, yy, part):
        ref = self.slot(xx, yy, part)
        pltpu.make_async_copy(ref, ref, self.xr.at[i, j, k]).wait()

    def rest(self):
        x, h, hn, xp, xm, x2 = self.x, self.h, self.hn, self.xp, self.xm, self.x2
        xs, xr = self.xs, self.xr
        for k in range(2):
            self.ysend[k].wait_recv()
            for i, dev in enumerate((self.xp_dev, self.xm_dev)):
                self.send(self.slot(x, hn, k), xs.at[i, 1, k], xr.at[i, 1, k], dev)
            self.to_core(x, hn, k)
        for j, yy in ((0, h), (1, hn)):
            for k in range(2):
                self.arrived(0, j, k, xm, yy, k)
                if k == 0:
                    self.send(self.slot(xm, yy, 0), xs.at[0, 2, j], xr.at[0, 2, j], self.xp_dev)
                self.to_core(xm, yy, k)
                self.arrived(1, j, k, xp, yy, k)
                if k == 1:
                    self.send(self.slot(xp, yy, 1), xs.at[1, 2, j], xr.at[1, 2, j], self.xm_dev)
                self.to_core(xp, yy, k)
        for j, yy in ((0, h), (1, hn)):
            self.arrived(0, 2, j, x2, yy, 0)
            self.to_core(x2, yy, 0)
            self.arrived(1, 2, j, x2, yy, 1)
            self.to_core(x2, yy, 1)
        for d in self.core:
            d.wait_recv()

    def drain(self):
        for d in self.started:
            d.wait_send()


def ring_sems():
    sem = pltpu.SemaphoreType.DMA
    return [sem((2,)), sem((2,)), sem((2, 3, 2)), sem((2, 3, 2)), sem((16,)), sem((16,))]


def seams(s, x, y, c):
    h = (y + (s % 8) // 7) % 2
    to_left = ((s + 15) % 16, bond(x, (y + ((s + 7) % 8) // 7) % 2, c))
    from_right = ((s + 1) % 16, bond(x, h, c))
    return h, to_left, from_right


def gather_kernel(own, out, zs, zr, *sems):
    s, x, y, c = place()
    h, to_left, from_right = seams(s, x, y, c)
    ring = Ring(out, sems, s, x, y, c, h)
    greet([from_right] + ring.partners, 5)
    z = []
    for k in range(2):
        d = rcopy(
            own.at[pl.ds(128 * k, 128)], out.at[c * 8 + x * 2 + y, pl.ds(128 * k, 128)],
            zs.at[k], zr.at[k], to_left,
        )
        d.start()
        z.append(d)
    for k in range(2):
        z[k].wait_recv()
        ring.home(k)
    ring.rest()
    for d in z:
        d.wait_send()
    ring.drain()


def gather(own, cid):
    sem = pltpu.SemaphoreType.DMA
    return pl.pallas_call(
        gather_kernel,
        name="gather%d" % cid,
        out_shape=jax.ShapeDtypeStruct((16, 256, CHI), BF16),
        in_specs=[ANY],
        out_specs=ANY,
        scratch_shapes=[sem((2,)), sem((2,))] + ring_sems(),
        compiler_params=params(cid),
    )(own)


BLOCKS = [(0, 0), (1, 0), (1, 1), (2, 0), (2, 1), (2, 2), (3, 0), (3, 1), (3, 2), (3, 3)]


def theta_kernel(a, b, proj, gate3, theta, sketch, pay, raw):
    a_val = a[...]

    def raw_step(t, _):
        cols = pl.ds(pl.multiple_of(t * CHI, CHI), CHI)
        rows = pl.ds(pl.multiple_of(t * 32, 32), 32)
        acc = None
        for c in range(2):
            part = jnp.concatenate(
                [b[(i % 2) * 8 + i // 2, rows, :] for i in range(8 * c, 8 * c + 8)], axis=0
            )
            term = jnp.dot(a_val[:, c * 256:(c + 1) * 256], part, preferred_element_type=F32)
            acc = term if acc is None else acc + term
        raw[:, cols] = acc
        return 0

    lax.fori_loop(0, PHYS, raw_step, 0)
    g3 = gate3[...]

    def gate_step(i, ss):
        halves = []
        for e in range(2):
            rows = pl.ds(pl.multiple_of(i * 16, 16) + 8 * e, 8)
            xr = jnp.concatenate(
                [raw[rows, t * CHI:(t + 1) * CHI] for t in range(PHYS)], axis=0
            )
            hi = xr.astype(BF16)
            lo = (xr - hi.astype(F32)).astype(BF16)
            x3 = jnp.concatenate([hi, lo, hi], axis=0)
            g = jnp.dot(g3, x3, preferred_element_type=F32)
            for v in range(PHYS):
                gv = g[v * 8:(v + 1) * 8, :]
                ss = ss + gv * gv
            halves.append(g)
        rows = pl.ds(pl.multiple_of(i * 16, 16), 16)
        for v in range(PHYS):
            pair = jnp.concatenate([h[v * 8:(v + 1) * 8, :] for h in halves], axis=0)
            theta[rows, v * CHI:(v + 1) * CHI] = pair.astype(BF16)
        return ss

    ss = lax.fori_loop(0, 16, gate_step, jnp.zeros((8, CHI), F32))
    ss = (ss[:, 0:128] + ss[:, 128:256]) + (ss[:, 256:384] + ss[:, 384:512])
    sk = jnp.dot(theta[...], proj[...], preferred_element_type=F32)
    sketch[...] = sk
    skt = sk.T
    for n, (bi, bj) in enumerate(BLOCKS):
        blk = lax.dot_general(
            skt[bi * 128:(bi + 1) * 128, :], sk[:, bj * 128:(bj + 1) * 128],
            (((1,), (0,)), ((), ())), precision=HI, preferred_element_type=F32,
        )
        r = 128 * n
        while r < 128 * n + 128:
            p, o = r // 80, r % 80
            e = min(80 - o, 128 * n + 128 - r)
            pay[p, o:o + e, :] = blk[r - 128 * n:r - 128 * n + e, :]
            r += e
    for p in range(16):
        pay[p, 80:88, :] = ss


def theta_call(a, b, proj, gate3):
    return pl.pallas_call(
        theta_kernel,
        name="theta",
        out_shape=[
            jax.ShapeDtypeStruct((256, PHYS * CHI), BF16),
            jax.ShapeDtypeStruct((256, CHI), F32),
            jax.ShapeDtypeStruct((16, 88, 128), F32),
        ],
        in_specs=[VMEM] * 4,
        out_specs=[VMEM] * 3,
        scratch_shapes=[pltpu.VMEM((256, PHYS * CHI), F32)],
        compiler_params=params(),
    )(a, b, proj, gate3)


def gram_kernel(pay, out, half, rb0, rb1, s0, r0, s1, r1, s2, r2, s3, r3):
    s, x, y, c = place()
    me = x * 2 + y
    c_dev = (s, bond(x, y, 1 - c))
    peers = []
    for k in range(1, 8):
        q = (me + k) % 8
        peers.append((k, q, (s, bond(q // 2, q % 2, c))))
    greet([c_dev] + [p[2] for p in peers], 8)

    first = rcopy(pay.at[pl.ds((1 - c) * 8, 8)], rb0, s0, r0, c_dev)
    first.start()
    first.wait_recv()
    half[...] = pay[pl.ds(c * 8, 8)] + rb0[...]
    sends = [first]
    recvs = []
    for k, q, dev in peers:
        d = rcopy(half.at[q], rb1.at[k - 1], s1.at[k - 1], r1.at[k - 1], dev)
        d.start()
        sends.append(d)
        recvs.append(d)
    acc = half[me]
    for d in recvs:
        d.wait_recv()
    t = [rb1[k] for k in range(7)]
    mine = ((acc + t[0]) + (t[1] + t[2])) + ((t[3] + t[4]) + (t[5] + t[6]))
    slot = c * 8 + me
    out[slot] = mine
    bcast = []
    for k, q, dev in peers:
        d = rcopy(out.at[slot], out.at[slot], s2.at[k - 1], r2.at[k - 1], dev)
        d.start()
        sends.append(d)
        bcast.append(d)
    core = []
    d = rcopy(out.at[slot], out.at[slot], s3.at[0], r3.at[0], c_dev)
    d.start()
    core.append(d)
    for k in range(1, 8):
        bcast[k - 1].wait_recv()
        src = c * 8 + (me + 8 - k) % 8
        d = rcopy(out.at[src], out.at[src], s3.at[k], r3.at[k], c_dev)
        d.start()
        core.append(d)
    for d in core:
        d.wait_recv()
    for d in sends + core:
        d.wait_send()


def gram_call(pay, cid):
    sem = pltpu.SemaphoreType.DMA
    return pl.pallas_call(
        gram_kernel,
        name="gram%d" % cid,
        out_shape=jax.ShapeDtypeStruct((16, 88, 128), F32),
        in_specs=[VMEM],
        out_specs=VMEM,
        scratch_shapes=[
            pltpu.VMEM((8, 88, 128), F32), pltpu.VMEM((8, 88, 128), F32),
            pltpu.VMEM((7, 88, 128), F32),
            sem, sem, sem((7,)), sem((7,)), sem((7,)), sem((7,)), sem((8,)), sem((8,)),
        ],
        compiler_params=params(cid),
    )(pay)


def bl(v, k):
    return jnp.broadcast_to(v[:, k:k + 1], (8, 128))


def bs(v, j):
    return jnp.broadcast_to(v[j:j + 1, :], (8, 128))


def leaf(rows):
    lane = lax.broadcasted_iota(jnp.int32, (8, 128), 1)
    sub = lax.broadcasted_iota(jnp.int32, (8, 128), 0)
    rows = list(rows)
    out = []
    n = len(rows)
    for p in range(n):
        m_p = rows[p]
        c = [bl(m_p, 8 * p + v) for v in range(8)]
        pc = (lane >= 8 * p) & (lane < 8 * p + 8)
        m_p = jnp.where(pc, jnp.where(lane - 8 * p == sub, 1.0, 0.0), m_p)
        fwd = m_p
        diag = None
        for j in range(8):
            d = bs(c[j], j)
            isj = sub == j
            mult = jnp.where(isj, 0.0, c[j] * (1.0 / d))
            if j:
                diag = jnp.where(isj, d, diag)
                fwd = jnp.where(isj, m_p, fwd)
            else:
                diag = d
            for v in range(j + 1, 8):
                c[v] = c[v] - mult * bs(c[v], j)
            m_p = m_p - mult * bs(m_p, j)
        out.append(jnp.where(lane < 8 * p + 8, fwd * lax.rsqrt(diag), 0.0))
        if p == n - 1:
            break
        yy = m_p * (1.0 / diag)
        yb = [bs(yy, v) for v in range(8)]
        for q in range(p + 1, n):
            t = [bl(rows[q], 8 * p + v) * yb[v] for v in range(8)]
            tot = ((t[0] + t[1]) + (t[2] + t[3])) + ((t[4] + t[5]) + (t[6] + t[7]))
            rows[q] = jnp.where(pc, 0.0, rows[q]) - tot
    return out


def dott(a, b):
    return lax.dot_general(
        a, b, (((1,), (1,)), ((), ())), precision=HI, preferred_element_type=F32
    )


def dotn(a, b):
    return lax.dot_general(
        a, b, (((1,), (0,)), ((), ())), precision=HI, preferred_element_type=F32
    )


def chol_body(a, linv):
    linv[...] = jnp.zeros_like(linv)
    for b in range(4):
        o = b * 128
        x = jnp.concatenate(leaf([a[o + 8 * q:o + 8 * q + 8, o:o + 128] for q in range(16)]), 0)
        linv[o:o + 128, o:o + 128] = x
        if b < 3:
            lb = dott(a[o + 128:, o:o + 128], x)
            a[o + 128:, o:o + 128] = lb
            a[o + 128:, o + 128:] = a[o + 128:, o + 128:] - dott(lb, lb)
        if b > 0:
            t = dotn(a[o:o + 128, :o], linv[:o, :o])
            linv[o:o + 128, :o] = -dotn(x, t)


def chol_kernel(pay, sketch, theta, left, leftp, thc, log, a, linv, ss, rs, own_sem):
    s, x, y, c = place()
    b = bond(x, y, c)
    peers = []
    for k in range(1, 16):
        q = (b + k) % 16
        peers.append((q, (s, q)))
    greet([p[1] for p in peers], 15)
    slot = c * 8 + x * 2 + y

    def columns(q):
        return theta.at[:, pl.ds(pl.multiple_of(q * 256, 256), 256)]

    own = pltpu.make_async_copy(columns(b), thc.at[slot], own_sem)
    own.start()
    moves = []
    for k, (q, dev) in enumerate(peers):
        d = rcopy(columns(q), thc.at[slot], ss.at[k], rs.at[k], dev)
        d.start()
        moves.append(d)
    for n, (bi, bj) in enumerate(BLOCKS):
        r = 128 * n
        while r < 128 * n + 128:
            p, o = r // 80, r % 80
            e = min(80 - o, 128 * n + 128 - r)
            q = bi * 128 + r - 128 * n
            a[q:q + e, bj * 128:(bj + 1) * 128] = pay[p, o:o + e, :]
            r += e
    chol_body(a, linv)
    root = math.sqrt(PHYS * CHI)
    ln = (dott(sketch[...], linv[...]) * root).astype(BF16)
    left[...] = ln
    ri = lax.broadcasted_iota(jnp.int32, (256, 256), 0)
    ci = lax.broadcasted_iota(jnp.int32, (256, 256), 1)
    perm = jnp.where(ci == (ri % 32) * 8 + ri // 32, 1.0, 0.0).astype(BF16)
    leftp[...] = jnp.dot(perm, ln, preferred_element_type=F32).astype(BF16)
    total = jnp.sum(jnp.sum(pay[0, 80:88, :], axis=0, keepdims=True), axis=1, keepdims=True)
    mean_square = total * (1.0 / (CHI * PHYS * PHYS * CHI)) + epsilon
    log[0:8, :] = jnp.broadcast_to(0.5 * jnp.log(mean_square), (8, 128))
    log[8:16, :] = jnp.broadcast_to(lax.rsqrt(mean_square) * (1.0 / root), (8, 128))
    own.wait()
    for d in moves:
        d.wait_recv()
    for d in moves:
        d.wait_send()


def chol_call(pay, sketch, theta, cid):
    sem = pltpu.SemaphoreType.DMA
    return pl.pallas_call(
        chol_kernel,
        name="chol%d" % cid,
        out_shape=[
            jax.ShapeDtypeStruct((256, CHI), BF16),
            jax.ShapeDtypeStruct((256, CHI), BF16),
            jax.ShapeDtypeStruct((16, 256, 256), BF16),
            jax.ShapeDtypeStruct((16, 128), F32),
        ],
        in_specs=[VMEM] * 3,
        out_specs=[VMEM] * 4,
        scratch_shapes=[
            pltpu.VMEM((CHI, CHI), F32), pltpu.VMEM((CHI, CHI), F32),
            sem((15,)), sem((15,)), sem,
        ],
        compiler_params=params(cid),
    )(pay, sketch, theta)


def tail_kernel(parity, last, left, leftp, thc, log, out, rcol, rsend, zs, zr, ls, as_, ar, *sems):
    s, x, y, c = place()
    is_left = s % 2 == parity
    h, to_left, from_right = seams(s, x, y, c)
    if last:
        h = y
    ring = Ring(out, sems, s, x, y, c, h)
    right, before = (s + 1) % 16, (s + 15) % 16
    targets = [(right, q) for q in range(16)]
    sources = [(before, q) for q in range(16)]
    greet(ring.partners + sources + ([] if last else [from_right]), 20 + (0 if last else 1))
    slot = c * 8 + x * 2 + y
    home = c * 8 + x * 2 + h

    def half(k):
        return pl.ds(128 * k, 128)

    if last:
        loc = [
            pltpu.make_async_copy(left.at[half(k)], out.at[slot, half(k)], ls.at[k])
            for k in range(2)
        ]
        for d in loc:
            d.start()
        for k in range(2):
            loc[k].wait()
            ring.home(k)
        ring.rest()
        ring.drain()
    else:
        loc = [
            pltpu.make_async_copy(left.at[half(k)], out.at[home, half(k)], ls.at[k])
            for k in range(2)
        ]
        z = [
            rcopy(leftp.at[half(k)], out.at[slot, half(k)], zs.at[k], zr.at[k], to_left)
            for k in range(2)
        ]

        @pl.when(is_left)
        def _():
            for k in range(2):
                loc[k].start()
                z[k].start()

        for k in range(2):
            @pl.when(is_left)
            def _():
                loc[k].wait()

            @pl.when(jnp.logical_not(is_left))
            def _():
                z[k].wait_recv()

            ring.home(k)
        ring.rest()

        @pl.when(is_left)
        def _():
            for k in range(2):
                z[k].wait_send()

        ring.drain()

    sends = [
        rcopy(rsend.at[q], rcol.at[bond(x, y, c)], as_.at[q], ar.at[bond(x, y, c)], targets[q])
        for q in range(16)
    ]

    @pl.when(is_left)
    def _():
        acc = lax.dot_general(
            out[...].reshape(4096, CHI), thc[...].reshape(4096, 256),
            (((0,), (0,)), ((), ())), preferred_element_type=F32,
        )
        blk = (acc * log[8:9, 0:1]).astype(BF16)
        for q in range(16):
            rsend[q] = blk[q * 32:(q + 1) * 32, :]
        for d in sends:
            d.start()
        for d in sends:
            d.wait_send()

    @pl.when(jnp.logical_not(is_left))
    def _():
        for q in range(16):
            pltpu.make_async_copy(rcol.at[q], rcol.at[q], ar.at[q]).wait()


def tail_call(left, leftp, thc, log, parity, cid):
    sem = pltpu.SemaphoreType.DMA
    return pl.pallas_call(
        functools.partial(tail_kernel, parity, parity == 1),
        name="tail%d" % cid,
        out_shape=[
            jax.ShapeDtypeStruct((16, 256, CHI), BF16),
            jax.ShapeDtypeStruct((16, 32, 256), BF16),
        ],
        in_specs=[VMEM] * 4,
        out_specs=[VMEM] * 2,
        scratch_shapes=[
            pltpu.VMEM((16, 32, 256), BF16),
            sem((2,)), sem((2,)), sem((2,)), sem((16,)), sem((16,)),
        ] + ring_sems(),
        compiler_params=params(cid),
    )(left, leftp, thc, log)


def gate_split(gates, position):
    g = lax.dynamic_index_in_dim(gates, position, 0, keepdims=False)
    g = g.reshape(8, 8, 8, 8).transpose(1, 0, 3, 2).reshape(64, 64)
    hi = lax.reduce_precision(g, 8, 7)
    lo = (g - hi).astype(BF16)
    hi = hi.astype(BF16)
    return jnp.concatenate([hi, hi, lo], axis=1)


def shards(mps, projection, gates):
    position = lax.axis_index("site")
    gate3 = gate_split(gates, position)
    proj = projection[0]
    b = gather(mps[0].transpose(1, 0, 2).reshape(256, CHI), 0)
    a = mps[0].reshape(256, CHI)
    logs, tensors = [], []
    for parity in range(2):
        theta, sketch, pay = theta_call(a, b, proj, gate3)
        pay = gram_call(pay, 3 * parity + 1)
        left, leftp, thc, log = chol_call(pay, sketch, theta, 3 * parity + 2)
        b, rcol = tail_call(left, leftp, thc, log, parity, 3 * parity + 3)
        a = rcol.reshape(PHYS, 2, 32, 256).transpose(2, 0, 1, 3).reshape(256, CHI)
        logs.append(log[0, 0:1])
        tensors.append(left)
    odd = position % 2 == 1
    state = jnp.where(odd, tensors[1], a).reshape(32, PHYS, CHI)
    return state[None], jnp.where(odd, logs[1], logs[0])


def solution(mesh):
    return jax.shard_map(
        shards,
        mesh=mesh,
        in_specs=(P("site", "bond", None, None), P("site", None, None), P()),
        out_specs=(P("site", "bond", None, None), P("site")),
        check_vma=False,
    )
```

profile of v0, /device:TPU:7, one launch (start us, length us, event | category | flops | bytes accessed | tf_op | source)
XLA Modules:
  0.0 282.2 jit_solution(13277266864886918750)
XLA Ops:
  0.6 0.0 copy-start
  0.7 1.0 copy-done
  1.7 0.1 reshape.28
  1.8 0.1 copy.9
  2.0 0.1 reshape.29
  2.1 0.7 pad_maximum_fusion.gate3
  2.8 1.7 copy.8
  4.5 30.4 %gather0.1.b = bf16[16,256,512]{2,1,0:T(8,128)(2,1)} custom-call(bf16[256,512]{1,0:T(8,128)(2,1)} %bitcast.27), custom_call_target="tpu_custom_call" | custom-call | tf_op jit(solution)/shard_map/gather0/pallas_call | solution.py:161
  34.9 12.5 %theta.2 = (bf16[256,4096]{1,0:T(8,128)(2,1)}, f32[256,512]{1,0:T(8,128)}, f32[16,88,128]{2,1,0:T(8,128)}) custom-call(bf16[256,512]{1,0:T(8,128)(2,1)} %bitcast.25, bf16[16,256,512]{2,1,0:T(8,128)(2,1)} %gather0.1.b, bf16[4096,512]{1,0:T(8,128)(2,1)} %bitcast.22, bf16[64,192]{1,0:T(8,128)(2,1)} %pad_maximum_fusion.gate3), custom_call_target="tpu_custom_call" | custom-call | tf_op jit(solution)/shard_map/theta/pallas_call | solution.py:236
  47.4 19.8 %gram1.1.pay = f32[16,88,128]{2,1,0:T(8,128)} custom-call(f32[16,88,128]{2,1,0:T(8,128)} %get-tuple-element.19.pay), custom_call_target="tpu_custom_call" | custom-call | tf_op jit(solution)/shard_map/gram1/pallas_call | solution.py:303
  67.3 35.3 %chol2.1 = (bf16[256,512]{1,0:T(8,128)(2,1)}, bf16[256,512]{1,0:T(8,128)(2,1)}, bf16[16,256,256]{2,1,0:T(8,128)(2,1)}, f32[16,128]{1,0:T(8,128)}) custom-call(f32[16,88,128]{2,1,0:T(8,128)} %gram1.1.pay, f32[256,512]{1,0:T(8,128)} %get-tuple-element.20.sketch, bf16[256,4096]{1,0:T(8,128)(2,1)} %get-tuple-element.21.theta), custom_call_target="tpu_custom_call" | custom-call | tf_op jit(solution)/shard_map/chol2/pallas_call | solution.py:439
  102.5 1.2 slice.7
  103.8 48.4 %tail3.1 = (bf16[16,256,512]{2,1,0:T(8,128)(2,1)}, bf16[16,32,256]{2,1,0:T(8,128)(2,1)}) custom-call(bf16[256,512]{1,0:T(8,128)(2,1)} %get-tuple-element.22.left, bf16[256,512]{1,0:T(8,128)(2,1)} %get-tuple-element.23.leftp, bf16[16,256,256]{2,1,0:T(8,128)(2,1)} %get-tuple-element.24.thc, f32[16,128]{1,0:T(8,128)} %get-tuple-element.25.log), custom_call_target="tpu_custom_call" | custom-call | tf_op jit(solution)/shard_map/tail3/pallas_call | solution.py:549
  152.1 1.8 copy.10
  153.9 12.5 %theta.3 = (bf16[256,4096]{1,0:T(8,128)(2,1)}, f32[256,512]{1,0:T(8,128)}, f32[16,88,128]{2,1,0:T(8,128)}) custom-call(bf16[256,512]{1,0:T(8,128)(2,1)} %bitcast.26, bf16[16,256,512]{2,1,0:T(8,128)(2,1)} %get-tuple-element.27.b, bf16[4096,512]{1,0:T(8,128)(2,1)} %bitcast.23, bf16[64,192]{1,0:T(8,128)(2,1)} %pad_maximum_fusion.gate3), custom_call_target="tpu_custom_call" | custom-call | tf_op jit(solution)/shard_map/theta/pallas_call | solution.py:236
  166.4 20.5 %gram4.1.pay = f32[16,88,128]{2,1,0:T(8,128)} custom-call(f32[16,88,128]{2,1,0:T(8,128)} %get-tuple-element.28.pay), custom_call_target="tpu_custom_call" | custom-call | tf_op jit(solution)/shard_map/gram4/pallas_call | solution.py:303
  186.9 35.2 %chol5.1 = (bf16[256,512]{1,0:T(8,128)(2,1)}, bf16[256,512]{1,0:T(8,128)(2,1)}, bf16[16,256,256]{2,1,0:T(8,128)(2,1)}, f32[16,128]{1,0:T(8,128)}) custom-call(f32[16,88,128]{2,1,0:T(8,128)} %gram4.1.pay, f32[256,512]{1,0:T(8,128)} %get-tuple-element.29.sketch, bf16[256,4096]{1,0:T(8,128)(2,1)} %get-tuple-element.30.theta), custom_call_target="tpu_custom_call" | custom-call | tf_op jit(solution)/shard_map/chol5/pallas_call | solution.py:439
  222.1 1.2 slice.6
  224.6 54.3 %tail6.1 = (bf16[16,256,512]{2,1,0:T(8,128)(2,1)}, bf16[16,32,256]{2,1,0:T(8,128)(2,1)}) custom-call(bf16[256,512]{1,0:T(8,128)(2,1)} %get-tuple-element.31.left, bf16[256,512]{1,0:T(8,128)(2,1)} %get-tuple-element.32.leftp, bf16[16,256,256]{2,1,0:T(8,128)(2,1)} %get-tuple-element.33.thc, f32[16,128]{1,0:T(8,128)} %get-tuple-element.34.log), custom_call_target="tpu_custom_call" | custom-call | tf_op jit(solution)/shard_map/tail6/pallas_call | solution.py:549
  278.9 1.1 copy.11
  280.0 0.8 select_bitcast_fusion
  (2 shorter events, 0.0 us)
Async XLA Ops:
  0.6 1.0 copy-start
where the time goes:
time: 286 us; the launch traced here: 282 us
  Pallas kernels  269 us (94%)
  local copies, waits for them, and re-layouts  8.46 us (3%)
  between operations  3.43 us (1%)
    pallas_call x2, Pallas kernels, tail_call(): pl.pallas_call(functools.partial(tail_kernel, parity, parity == 1), name=...  103 us
    pallas_call x2, Pallas kernels, chol_call(): pl.pallas_call(chol_kernel, name='chol%d' % cid, out_shape=[jax.ShapeDtyp...  70.5 us
    pallas_call x2, Pallas kernels, gram_call(): pl.pallas_call(gram_kernel, name='gram%d' % cid, out_shape=jax.ShapeDtype...  40.3 us
    pallas_call x1, Pallas kernels, gather(): pl.pallas_call(gather_kernel, name='gather%d' % cid, out_shape=jax.ShapeD...  30.4 us
    pallas_call x2, Pallas kernels, theta_call(): pl.pallas_call(theta_kernel, name='theta', out_shape=[jax.ShapeDtypeStruc...  25 us

commit v1 on v0

--- a/solution.py
+++ b/solution.py
@@ -180,9 +180,14 @@
         rows = pl.ds(pl.multiple_of(t * 32, 32), 32)
         acc = None
         for c in range(2):
-            part = jnp.concatenate(
-                [b[(i % 2) * 8 + i // 2, rows, :] for i in range(8 * c, 8 * c + 8)], axis=0
-            )
+            slots = [(i % 2) * 8 + i // 2 for i in range(8 * c, 8 * c + 8)]
+            if len(b.shape) == 3:
+                part = jnp.concatenate([b[i, rows, :] for i in slots], axis=0)
+            else:
+                part = jnp.concatenate(
+                    [jnp.concatenate([b[k, i, rows, :] for i in slots], axis=0) for k in range(4)],
+                    axis=1,
+                )
             term = jnp.dot(a_val[:, c * 256:(c + 1) * 256], part, preferred_element_type=F32)
             acc = term if acc is None else acc + term
         raw[:, cols] = acc
@@ -323,7 +328,7 @@
     return jnp.broadcast_to(v[j:j + 1, :], (8, 128))
 
 
-def leaf(rows):
+def leaf(rows, hook):
     lane = lax.broadcasted_iota(jnp.int32, (8, 128), 1)
     sub = lax.broadcasted_iota(jnp.int32, (8, 128), 0)
     rows = list(rows)
@@ -357,6 +362,7 @@
             t = [bl(rows[q], 8 * p + v) * yb[v] for v in range(8)]
             tot = ((t[0] + t[1]) + (t[2] + t[3])) + ((t[4] + t[5]) + (t[6] + t[7]))
             rows[q] = jnp.where(pc, 0.0, rows[q]) - tot
+        hook(p)
     return out
 
 
@@ -372,41 +378,7 @@
     )
 
 
-def chol_body(a, linv):
-    linv[...] = jnp.zeros_like(linv)
-    for b in range(4):
-        o = b * 128
-        x = jnp.concatenate(leaf([a[o + 8 * q:o + 8 * q + 8, o:o + 128] for q in range(16)]), 0)
-        linv[o:o + 128, o:o + 128] = x
-        if b < 3:
-            lb = dott(a[o + 128:, o:o + 128], x)
-            a[o + 128:, o:o + 128] = lb
-            a[o + 128:, o + 128:] = a[o + 128:, o + 128:] - dott(lb, lb)
-        if b > 0:
-            t = dotn(a[o:o + 128, :o], linv[:o, :o])
-            linv[o:o + 128, :o] = -dotn(x, t)
-
-
-def chol_kernel(pay, sketch, theta, left, leftp, thc, log, a, linv, ss, rs, own_sem):
-    s, x, y, c = place()
-    b = bond(x, y, c)
-    peers = []
-    for k in range(1, 16):
-        q = (b + k) % 16
-        peers.append((q, (s, q)))
-    greet([p[1] for p in peers], 15)
-    slot = c * 8 + x * 2 + y
-
-    def columns(q):
-        return theta.at[:, pl.ds(pl.multiple_of(q * 256, 256), 256)]
-
-    own = pltpu.make_async_copy(columns(b), thc.at[slot], own_sem)
-    own.start()
-    moves = []
-    for k, (q, dev) in enumerate(peers):
-        d = rcopy(columns(q), thc.at[slot], ss.at[k], rs.at[k], dev)
-        d.start()
-        moves.append(d)
+def unpack_gram(pay, a):
     for n, (bi, bj) in enumerate(BLOCKS):
         r = 128 * n
         while r < 128 * n + 128:
@@ -415,152 +387,197 @@
             q = bi * 128 + r - 128 * n
             a[q:q + e, bj * 128:(bj + 1) * 128] = pay[p, o:o + e, :]
             r += e
-    chol_body(a, linv)
+
+
+def mid_kernel(parity, *refs):
+    first = parity == 0
+    refs = list(refs)
+    pay, sketch, theta, left, rcol, log = refs[:6]
+    refs = refs[6:]
+    if first:
+        bout, lp, zs, zr, gxs, gxr, gcs, gcr = refs[:1] + refs[-7:]
+        refs = refs[1:-7]
+    a, linv, part, rbc, rbd, fin = refs[:6]
+    cs, cr, ds, dr, as_, ar = refs[6:]
+
+    s, x, y, c = place()
+    is_left = s % 2 == parity
+    _, to_left, from_right = seams(s, x, y, c)
+    c_dev = (s, bond(x, y, 1 - c))
+    right, before = (s + 1) % 16, (s + 15) % 16
+    others = [(x * 2 + y + k) % 8 for k in range(1, 8)]
+    greet(
+        [c_dev] + [(s, bond(q // 2, q % 2, c)) for q in others]
+        + [(before, q) for q in range(16)] + ([from_right] if first else []),
+        25 if first else 24,
+    )
+    me = c * 8 + x * 2 + y
     root = math.sqrt(PHYS * CHI)
-    ln = (dott(sketch[...], linv[...]) * root).astype(BF16)
-    left[...] = ln
-    ri = lax.broadcasted_iota(jnp.int32, (256, 256), 0)
-    ci = lax.broadcasted_iota(jnp.int32, (256, 256), 1)
-    perm = jnp.where(ci == (ri % 32) * 8 + ri // 32, 1.0, 0.0).astype(BF16)
-    leftp[...] = jnp.dot(perm, ln, preferred_element_type=F32).astype(BF16)
-    total = jnp.sum(jnp.sum(pay[0, 80:88, :], axis=0, keepdims=True), axis=1, keepdims=True)
-    mean_square = total * (1.0 / (CHI * PHYS * PHYS * CHI)) + epsilon
-    log[0:8, :] = jnp.broadcast_to(0.5 * jnp.log(mean_square), (8, 128))
-    log[8:16, :] = jnp.broadcast_to(lax.rsqrt(mean_square) * (1.0 / root), (8, 128))
-    own.wait()
-    for d in moves:
-        d.wait_recv()
-    for d in moves:
-        d.wait_send()
-
-
-def chol_call(pay, sketch, theta, cid):
+
+    @pl.when(is_left)
+    def _():
+        sent = []
+
+        def send(src, dst, ss, rs, dev):
+            d = rcopy(src, dst, ss, rs, dev)
+            d.start()
+            sent.append(d)
+            return d
+
+        total = jnp.sum(jnp.sum(pay[0, 80:88, :], axis=0, keepdims=True), axis=1, keepdims=True)
+        mean_square = total * (1.0 / (CHI * PHYS * PHYS * CHI)) + epsilon
+        log[...] = jnp.broadcast_to(0.5 * jnp.log(mean_square), (8, 128))
+        scale = lax.rsqrt(mean_square) * (1.0 / root)
+        unpack_gram(pay, a)
+        ri = lax.broadcasted_iota(jnp.int32, (256, 256), 0)
+        ci = lax.broadcasted_iota(jnp.int32, (256, 256), 1)
+        perm = jnp.where(ci == (ri % 32) * 8 + ri // 32, 1.0, 0.0).astype(BF16)
+        core, peers = {}, {}
+
+        def publish(b):
+            o = b * 128
+            ln = (dott(sketch[:, :o + 128], linv[o:o + 128, :o + 128]) * root).astype(BF16)
+            left[:, o:o + 128] = ln
+            if first:
+                lp[b] = jnp.dot(perm, ln, preferred_element_type=F32).astype(BF16)
+                send(lp.at[b], bout.at[b, me], zs.at[b], zr.at[b], to_left)
+            lnt = ln.astype(F32).T.astype(BF16)
+            for t in range(PHYS):
+                blk = jnp.dot(
+                    lnt, theta[:, t * CHI:(t + 1) * CHI], preferred_element_type=F32
+                )
+                blk = (blk * scale).astype(BF16)
+                part[b, 2 * t] = blk[:, 0:256]
+                part[b, 2 * t + 1] = blk[:, 256:512]
+            core[b] = send(
+                part.at[b, pl.ds((1 - c) * 8, 8)], rbc.at[b], cs.at[b], cr.at[b], c_dev
+            )
+
+        def step_a(b):
+            core[b].wait_recv()
+            half = part[b, pl.ds(c * 8, 8)].astype(F32) + rbc[b].astype(F32)
+            part[b, pl.ds(c * 8, 8)] = half.astype(BF16)
+            peers[b] = [
+                send(
+                    part.at[b, c * 8 + q], rbd.at[b, k], ds.at[b, k], dr.at[b, k],
+                    (s, bond(q // 2, q % 2, c)),
+                )
+                for k, q in enumerate(others)
+            ]
+
+        def step_d(b):
+            for d in peers[b]:
+                d.wait_recv()
+            t = [rbd[b, k].astype(F32) for k in range(7)]
+            tot = ((part[b, me].astype(F32) + t[0]) + (t[1] + t[2])) + (
+                (t[3] + t[4]) + (t[5] + t[6]))
+            fin[b] = tot.astype(BF16)
+            for i in range(4):
+                send(
+                    fin.at[b, pl.ds(32 * i, 32)], rcol.at[me], as_.at[b, i], ar.at[me],
+                    (right, 4 * b + i),
+                )
+
+        plan = {
+            1: {9: [(step_a, 0)]},
+            2: {9: [(step_a, 1)], 13: [(step_d, 0)]},
+            3: {9: [(step_a, 2)], 13: [(step_d, 1)]},
+        }
+        for b in range(4):
+            o = b * 128
+            t = dotn(a[o:o + 128, :o], linv[:o, :o]) if b else None
+
+            def hook(p, b=b):
+                for f, arg in plan.get(b, {}).get(p, ()):
+                    f(arg)
+
+            inv = jnp.concatenate(
+                leaf([a[o + 8 * q:o + 8 * q + 8, o:o + 128] for q in range(16)], hook), 0
+            )
+            linv[o:o + 128, o:o + 128] = inv
+            if b < 3:
+                linv[o:o + 128, o + 128:] = jnp.zeros((128, CHI - o - 128), F32)
+            if b > 0:
+                linv[o:o + 128, :o] = -dotn(inv, t)
+            publish(b)
+            if b < 3:
+                lb = dott(a[o + 128:, o:o + 128], inv)
+                a[o + 128:, o:o + 128] = lb
+                a[o + 128:, o + 128:] = a[o + 128:, o + 128:] - dott(lb, lb)
+        step_a(3)
+        step_d(2)
+        step_d(3)
+        for d in sent:
+            d.wait_send()
+
+    @pl.when(jnp.logical_not(is_left))
+    def _():
+        if first:
+            seam = (s % 8) // 7
+            sent, cores = [], []
+
+            def slot(b, q):
+                return bout.at[b, c * 8 + (q // 2) * 2 + (q % 2 + seam) % 2]
+
+            def send(ref, ss, rs, dev):
+                d = rcopy(ref, ref, ss, rs, dev)
+                d.start()
+                sent.append(d)
+                return d
+
+            def here(ref, rs):
+                pltpu.make_async_copy(ref, ref, rs).wait()
+
+            mine = x * 2 + y
+            for b in range(5):
+                if b < 4:
+                    ref = slot(b, mine)
+                    here(ref, zr.at[b])
+                    for k, q in enumerate(others):
+                        send(ref, gxs.at[b, k], gxr.at[b, k], (s, bond(q // 2, q % 2, c)))
+                    cores.append(send(ref, gcs.at[b, 7], gcr.at[b, 7], c_dev))
+                if b > 0:
+                    for k in range(7):
+                        ref = slot(b - 1, (mine + 7 - k) % 8)
+                        here(ref, gxr.at[b - 1, k])
+                        cores.append(send(ref, gcs.at[b - 1, k], gcr.at[b - 1, k], c_dev))
+            for d in cores:
+                d.wait_recv()
+            for d in sent:
+                d.wait_send()
+        for q in range(16):
+            pltpu.make_async_copy(rcol.at[q], rcol.at[q], ar.at[q]).wait()
+
+
+def mid_call(pay, sketch, theta, parity, cid):
     sem = pltpu.SemaphoreType.DMA
+    first = parity == 0
+    outs = [
+        jax.ShapeDtypeStruct((256, CHI), BF16),
+        jax.ShapeDtypeStruct((16, 32, 256), BF16),
+        jax.ShapeDtypeStruct((8, 128), F32),
+    ]
+    scratch = [
+        pltpu.VMEM((CHI, CHI), F32), pltpu.VMEM((CHI, CHI), F32),
+        pltpu.VMEM((4, 16, 128, 256), BF16), pltpu.VMEM((4, 8, 128, 256), BF16),
+        pltpu.VMEM((4, 7, 128, 256), BF16), pltpu.VMEM((4, 128, 256), BF16),
+        sem((4,)), sem((4,)), sem((4, 7)), sem((4, 7)), sem((4, 4)), sem((16,)),
+    ]
+    if first:
+        outs.append(jax.ShapeDtypeStruct((4, 16, 256, 128), BF16))
+        scratch += [
+            pltpu.VMEM((4, 256, 128), BF16), sem((4,)), sem((4,)),
+            sem((4, 7)), sem((4, 7)), sem((4, 8)), sem((4, 8)),
+        ]
     return pl.pallas_call(
-        chol_kernel,
-        name="chol%d" % cid,
-        out_shape=[
-            jax.ShapeDtypeStruct((256, CHI), BF16),
-            jax.ShapeDtypeStruct((256, CHI), BF16),
-            jax.ShapeDtypeStruct((16, 256, 256), BF16),
-            jax.ShapeDtypeStruct((16, 128), F32),
-        ],
+        functools.partial(mid_kernel, parity),
+        name="mid%d" % cid,
+        out_shape=outs,
         in_specs=[VMEM] * 3,
-        out_specs=[VMEM] * 4,
-        scratch_shapes=[
-            pltpu.VMEM((CHI, CHI), F32), pltpu.VMEM((CHI, CHI), F32),
-            sem((15,)), sem((15,)), sem,
-        ],
+        out_specs=[VMEM] * len(outs),
+        scratch_shapes=scratch,
         compiler_params=params(cid),
     )(pay, sketch, theta)
-
-
-def tail_kernel(parity, last, left, leftp, thc, log, out, rcol, rsend, zs, zr, ls, as_, ar, *sems):
-    s, x, y, c = place()
-    is_left = s % 2 == parity
-    h, to_left, from_right = seams(s, x, y, c)
-    if last:
-        h = y
-    ring = Ring(out, sems, s, x, y, c, h)
-    right, before = (s + 1) % 16, (s + 15) % 16
-    targets = [(right, q) for q in range(16)]
-    sources = [(before, q) for q in range(16)]
-    greet(ring.partners + sources + ([] if last else [from_right]), 20 + (0 if last else 1))
-    slot = c * 8 + x * 2 + y
-    home = c * 8 + x * 2 + h
-
-    def half(k):
-        return pl.ds(128 * k, 128)
-
-    if last:
-        loc = [
-            pltpu.make_async_copy(left.at[half(k)], out.at[slot, half(k)], ls.at[k])
-            for k in range(2)
-        ]
-        for d in loc:
-            d.start()
-        for k in range(2):
-            loc[k].wait()
-            ring.home(k)
-        ring.rest()
-        ring.drain()
-    else:
-        loc = [
-            pltpu.make_async_copy(left.at[half(k)], out.at[home, half(k)], ls.at[k])
-            for k in range(2)
-        ]
-        z = [
-            rcopy(leftp.at[half(k)], out.at[slot, half(k)], zs.at[k], zr.at[k], to_left)
-            for k in range(2)
-        ]
-
-        @pl.when(is_left)
-        def _():
-            for k in range(2):
-                loc[k].start()
-                z[k].start()
-
-        for k in range(2):
-            @pl.when(is_left)
-            def _():
-                loc[k].wait()
-
-            @pl.when(jnp.logical_not(is_left))
-            def _():
-                z[k].wait_recv()
-
-            ring.home(k)
-        ring.rest()
-
-        @pl.when(is_left)
-        def _():
-            for k in range(2):
-                z[k].wait_send()
-
-        ring.drain()
-
-    sends = [
-        rcopy(rsend.at[q], rcol.at[bond(x, y, c)], as_.at[q], ar.at[bond(x, y, c)], targets[q])
-        for q in range(16)
-    ]
-
-    @pl.when(is_left)
-    def _():
-        acc = lax.dot_general(
-            out[...].reshape(4096, CHI), thc[...].reshape(4096, 256),
-            (((0,), (0,)), ((), ())), preferred_element_type=F32,
-        )
-        blk = (acc * log[8:9, 0:1]).astype(BF16)
-        for q in range(16):
-            rsend[q] = blk[q * 32:(q + 1) * 32, :]
-        for d in sends:
-            d.start()
-        for d in sends:
-            d.wait_send()
-
-    @pl.when(jnp.logical_not(is_left))
-    def _():
-        for q in range(16):
-            pltpu.make_async_copy(rcol.at[q], rcol.at[q], ar.at[q]).wait()
-
-
-def tail_call(left, leftp, thc, log, parity, cid):
-    sem = pltpu.SemaphoreType.DMA
-    return pl.pallas_call(
-        functools.partial(tail_kernel, parity, parity == 1),
-        name="tail%d" % cid,
-        out_shape=[
-            jax.ShapeDtypeStruct((16, 256, CHI), BF16),
-            jax.ShapeDtypeStruct((16, 32, 256), BF16),
-        ],
-        in_specs=[VMEM] * 4,
-        out_specs=[VMEM] * 2,
-        scratch_shapes=[
-            pltpu.VMEM((16, 32, 256), BF16),
-            sem((2,)), sem((2,)), sem((2,)), sem((16,)), sem((16,)),
-        ] + ring_sems(),
-        compiler_params=params(cid),
-    )(left, leftp, thc, log)
 
 
 def gate_split(gates, position):
@@ -582,8 +599,8 @@
     for parity in range(2):
         theta, sketch, pay = theta_call(a, b, proj, gate3)
         pay = gram_call(pay, 3 * parity + 1)
-        left, leftp, thc, log = chol_call(pay, sketch, theta, 3 * parity + 2)
-        b, rcol = tail_call(left, leftp, thc, log, parity, 3 * parity + 3)
+        left, rcol, log, *more = mid_call(pay, sketch, theta, parity, 3 * parity + 2)
+        b = more[0] if more else None
         a = rcol.reshape(PHYS, 2, 32, 256).transpose(2, 0, 1, 3).reshape(256, CHI)
         logs.append(log[0, 0:1])
         tensors.append(left)

time: 286 us -> 228 us (0.80)
  Pallas kernels: 269 us -> 210 us
    pallas_call x4 -> x2, Pallas kernels: 173 us -> 114 us  [mid_call(): pl.pallas_call(functools.partial(mid_kernel, parity), name='mid%d' % cid,...]
where the time goes in v1:
time: 228 us; the launch traced here: 224 us
  Pallas kernels  210 us (92%)
  local copies, waits for them, and re-layouts  8.42 us (4%)
  between operations  3.39 us (1%)
    pallas_call x2, Pallas kernels, mid_call(): pl.pallas_call(functools.partial(mid_kernel, parity), name='mid%d' % cid,...  114 us
    pallas_call x2, Pallas kernels, gram_call(): pl.pallas_call(gram_kernel, name='gram%d' % cid, out_shape=jax.ShapeDtype...  40.9 us
    pallas_call x1, Pallas kernels, gather(): pl.pallas_call(gather_kernel, name='gather%d' % cid, out_shape=jax.ShapeD...  30.4 us
    pallas_call x2, Pallas kernels, theta_call(): pl.pallas_call(theta_kernel, name='theta', out_shape=[jax.ShapeDtypeStruc...  25 us

profile of v1, /device:TPU:7, one launch (start us, length us, event | category | flops | bytes accessed | tf_op | source)
XLA Modules:
  0.0 223.5 jit_solution(10469130717907643324)
XLA Ops:
  0.6 0.0 copy-start
  0.7 1.0 copy-done
  1.7 0.1 reshape.28
  1.8 0.1 copy.9
  2.0 0.1 reshape.29
  2.1 0.7 pad_maximum_fusion.gate3
  2.8 1.7 copy.8
  4.5 30.4 %gather0.1.b = bf16[16,256,512]{2,1,0:T(8,128)(2,1)} custom-call(bf16[256,512]{1,0:T(8,128)(2,1)} %bitcast.27), custom_call_target="tpu_custom_call" | custom-call | tf_op jit(solution)/shard_map/gather0/pallas_call | solution.py:161
  34.9 12.5 %theta.2 = (bf16[256,4096]{1,0:T(8,128)(2,1)}, f32[256,512]{1,0:T(8,128)}, f32[16,88,128]{2,1,0:T(8,128)}) custom-call(bf16[256,512]{1,0:T(8,128)(2,1)} %bitcast.25, bf16[16,256,512]{2,1,0:T(8,128)(2,1)} %gather0.1.b, bf16[4096,512]{1,0:T(8,128)(2,1)} %bitcast.22, bf16[64,192]{1,0:T(8,128)(2,1)} %pad_maximum_fusion.gate3), custom_call_target="tpu_custom_call" | custom-call | tf_op jit(solution)/shard_map/theta/pallas_call | solution.py:241
  47.4 19.8 %gram1.1.refs_0_ = f32[16,88,128]{2,1,0:T(8,128)} custom-call(f32[16,88,128]{2,1,0:T(8,128)} %get-tuple-element.14.pay), custom_call_target="tpu_custom_call" | custom-call | tf_op jit(solution)/shard_map/gram1/pallas_call | solution.py:308
  67.2 56.2 %mid2.1 = (bf16[256,512]{1,0:T(8,128)(2,1)}, bf16[16,32,256]{2,1,0:T(8,128)(2,1)}, f32[8,128]{1,0:T(8,128)}, bf16[4,16,256,128]{3,2,1,0:T(8,128)(2,1)}) custom-call(f32[16,88,128]{2,1,0:T(8,128)} %gram1.1.refs_0_, f32[256,512]{1,0:T(8,128)} %get-tuple-element.15.refs_1_, bf16[256,4096]{1,0:T(8,128)(2,1)} %get-tuple-element.16.refs_2_), custom_call_target="tpu_custom_call" | custom-call | tf_op jit(solution)/shard_map/mid2/pallas_call | solution.py:572
  123.4 1.2 slice.7
  124.6 1.8 copy.10
  126.4 12.5 %theta.3 = (bf16[256,4096]{1,0:T(8,128)(2,1)}, f32[256,512]{1,0:T(8,128)}, f32[16,88,128]{2,1,0:T(8,128)}) custom-call(bf16[256,512]{1,0:T(8,128)(2,1)} %bitcast.26, bf16[4,16,256,128]{3,2,1,0:T(8,128)(2,1)} %get-tuple-element.18.b, bf16[4096,512]{1,0:T(8,128)(2,1)} %bitcast.23, bf16[64,192]{1,0:T(8,128)(2,1)} %pad_maximum_fusion.gate3), custom_call_target="tpu_custom_call" | custom-call | tf_op jit(solution)/shard_map/theta/pallas_call | solution.py:241
  138.9 21.1 %gram4.1.refs_0_ = f32[16,88,128]{2,1,0:T(8,128)} custom-call(f32[16,88,128]{2,1,0:T(8,128)} %get-tuple-element.19.pay), custom_call_target="tpu_custom_call" | custom-call | tf_op jit(solution)/shard_map/gram4/pallas_call | solution.py:308
  160.0 57.8 %mid5.1 = (bf16[256,512]{1,0:T(8,128)(2,1)}, bf16[16,32,256]{2,1,0:T(8,128)(2,1)}, f32[8,128]{1,0:T(8,128)}) custom-call(f32[16,88,128]{2,1,0:T(8,128)} %gram4.1.refs_0_, f32[256,512]{1,0:T(8,128)} %get-tuple-element.20.refs_1_, bf16[256,4096]{1,0:T(8,128)(2,1)} %get-tuple-element.21.refs_2_), custom_call_target="tpu_custom_call" | custom-call | tf_op jit(solution)/shard_map/mid5/pallas_call | solution.py:572
  217.8 1.2 slice.6
  220.3 1.1 copy.11
  221.4 0.8 select_bitcast_fusion
  (2 shorter events, 0.0 us)
Async XLA Ops:
  0.6 1.0 copy-start

commit v2 on v1

--- a/solution.py
+++ b/solution.py
@@ -43,6 +43,15 @@
     for dev in sends_to_me:
         pl.semaphore_signal(barrier, inc=1, device_id=dev, device_id_type=MESH)
     pl.semaphore_wait(barrier, count)
+
+
+def swap_rows(value, inner):
+    n = value.shape[0]
+    ri = lax.broadcasted_iota(jnp.int32, (n, n), 0)
+    ci = lax.broadcasted_iota(jnp.int32, (n, n), 1)
+    outer = n // inner
+    perm = jnp.where(ci == (ri % outer) * inner + ri // outer, 1.0, 0.0).astype(BF16)
+    return jnp.dot(perm, value, preferred_element_type=F32).astype(BF16)
 
 
 def rcopy(src, dst, ssem, rsem, dev):
@@ -134,10 +143,11 @@
     return h, to_left, from_right
 
 
-def gather_kernel(own, out, zs, zr, *sems):
+def gather_kernel(mine, out, own, zs, zr, *sems):
     s, x, y, c = place()
     h, to_left, from_right = seams(s, x, y, c)
     ring = Ring(out, sems, s, x, y, c, h)
+    own[...] = swap_rows(mine[...], PHYS)
     greet([from_right] + ring.partners, 5)
     z = []
     for k in range(2):
@@ -162,9 +172,9 @@
         gather_kernel,
         name="gather%d" % cid,
         out_shape=jax.ShapeDtypeStruct((16, 256, CHI), BF16),
-        in_specs=[ANY],
+        in_specs=[VMEM],
         out_specs=ANY,
-        scratch_shapes=[sem((2,)), sem((2,))] + ring_sems(),
+        scratch_shapes=[pltpu.VMEM((256, CHI), BF16), sem((2,)), sem((2,))] + ring_sems(),
         compiler_params=params(cid),
     )(own)
 
@@ -172,7 +182,7 @@
 BLOCKS = [(0, 0), (1, 0), (1, 1), (2, 0), (2, 1), (2, 2), (3, 0), (3, 1), (3, 2), (3, 3)]
 
 
-def theta_kernel(a, b, proj, gate3, theta, sketch, pay, raw):
+def theta_kernel(a, b, proj, gates, theta, sketch, pay_a, pay_b, raw):
     a_val = a[...]
 
     def raw_step(t, _):
@@ -194,7 +204,14 @@
         return 0
 
     lax.fori_loop(0, PHYS, raw_step, 0)
-    g3 = gate3[...]
+    gate = gates[lax.axis_index("site")]
+    g_hi = gate.astype(BF16)
+    g_lo = (gate - g_hi.astype(F32)).astype(BF16)
+    g_hi, g_lo = [
+        swap_rows(swap_rows(g, 8).astype(F32).T.astype(BF16), 8).astype(F32).T.astype(BF16)
+        for g in (g_hi, g_lo)
+    ]
+    g3 = jnp.concatenate([g_hi, g_hi, g_lo], axis=1)
 
     def gate_step(i, ss):
         halves = []
@@ -227,97 +244,89 @@
             skt[bi * 128:(bi + 1) * 128, :], sk[:, bj * 128:(bj + 1) * 128],
             (((1,), (0,)), ((), ())), precision=HI, preferred_element_type=F32,
         )
-        r = 128 * n
-        while r < 128 * n + 128:
-            p, o = r // 80, r % 80
-            e = min(80 - o, 128 * n + 128 - r)
-            pay[p, o:o + e, :] = blk[r - 128 * n:r - 128 * n + e, :]
+        if n == 0:
+            for p in range(16):
+                pay_a[p, 0:8, :] = blk[8 * p:8 * p + 8, :]
+            continue
+        r = 128 * (n - 1)
+        while r < 128 * n:
+            p, o = r // 72, r % 72
+            e = min(72 - o, 128 * n - r)
+            pay_b[p, o:o + e, :] = blk[r - 128 * (n - 1):r - 128 * (n - 1) + e, :]
             r += e
     for p in range(16):
-        pay[p, 80:88, :] = ss
-
-
-def theta_call(a, b, proj, gate3):
+        pay_a[p, 8:16, :] = ss
+
+
+def theta_call(a, b, proj, gates):
     return pl.pallas_call(
         theta_kernel,
         name="theta",
         out_shape=[
             jax.ShapeDtypeStruct((256, PHYS * CHI), BF16),
             jax.ShapeDtypeStruct((256, CHI), F32),
-            jax.ShapeDtypeStruct((16, 88, 128), F32),
+            jax.ShapeDtypeStruct((16, 16, 128), F32),
+            jax.ShapeDtypeStruct((16, 72, 128), F32),
         ],
         in_specs=[VMEM] * 4,
-        out_specs=[VMEM] * 3,
+        out_specs=[VMEM] * 4,
         scratch_shapes=[pltpu.VMEM((256, PHYS * CHI), F32)],
         compiler_params=params(),
-    )(a, b, proj, gate3)
-
-
-def gram_kernel(pay, out, half, rb0, rb1, s0, r0, s1, r1, s2, r2, s3, r3):
-    s, x, y, c = place()
-    me = x * 2 + y
-    c_dev = (s, bond(x, y, 1 - c))
-    peers = []
-    for k in range(1, 8):
-        q = (me + k) % 8
-        peers.append((k, q, (s, bond(q // 2, q % 2, c))))
-    greet([c_dev] + [p[2] for p in peers], 8)
-
-    first = rcopy(pay.at[pl.ds((1 - c) * 8, 8)], rb0, s0, r0, c_dev)
-    first.start()
-    first.wait_recv()
-    half[...] = pay[pl.ds(c * 8, 8)] + rb0[...]
-    sends = [first]
-    recvs = []
-    for k, q, dev in peers:
-        d = rcopy(half.at[q], rb1.at[k - 1], s1.at[k - 1], r1.at[k - 1], dev)
+    )(a, b, proj, gates)
+
+
+class Sum:
+    def __init__(self, pay, half, rb0, rb1, out, sems, c, me, c_dev, devs, sent):
+        self.pay, self.half, self.rb0, self.rb1, self.out = pay, half, rb0, rb1, out
+        self.sems, self.c, self.me, self.c_dev, self.devs = sems, c, me, c_dev, devs
+        self.sent, self.cores = sent, []
+
+    def send(self, src, dst, i, k, dev):
+        d = rcopy(src, dst, self.sems[2 * i].at[k], self.sems[2 * i + 1].at[k], dev)
         d.start()
-        sends.append(d)
-        recvs.append(d)
-    acc = half[me]
-    for d in recvs:
-        d.wait_recv()
-    t = [rb1[k] for k in range(7)]
-    mine = ((acc + t[0]) + (t[1] + t[2])) + ((t[3] + t[4]) + (t[5] + t[6]))
-    slot = c * 8 + me
-    out[slot] = mine
-    bcast = []
-    for k, q, dev in peers:
-        d = rcopy(out.at[slot], out.at[slot], s2.at[k - 1], r2.at[k - 1], dev)
-        d.start()
-        sends.append(d)
-        bcast.append(d)
-    core = []
-    d = rcopy(out.at[slot], out.at[slot], s3.at[0], r3.at[0], c_dev)
-    d.start()
-    core.append(d)
-    for k in range(1, 8):
-        bcast[k - 1].wait_recv()
-        src = c * 8 + (me + 8 - k) % 8
-        d = rcopy(out.at[src], out.at[src], s3.at[k], r3.at[k], c_dev)
-        d.start()
-        core.append(d)
-    for d in core:
-        d.wait_recv()
-    for d in sends + core:
-        d.wait_send()
-
-
-def gram_call(pay, cid):
+        self.sent.append(d)
+        return d
+
+    def begin(self):
+        self.core = self.send(self.pay.at[pl.ds((1 - self.c) * 8, 8)], self.rb0, 0, 0, self.c_dev)
+
+    def scatter(self):
+        self.core.wait_recv()
+        self.half[...] = self.pay[pl.ds(self.c * 8, 8)] + self.rb0[...]
+        self.parts = [
+            self.send(self.half.at[(self.me + k + 1) % 8], self.rb1.at[k], 1, k, dev)
+            for k, dev in enumerate(self.devs)
+        ]
+
+    def spread(self):
+        for d in self.parts:
+            d.wait_recv()
+        t = [self.rb1[k] for k in range(7)]
+        slot = self.c * 8 + self.me
+        self.out[slot] = ((self.half[self.me] + t[0]) + (t[1] + t[2])) + (
+            (t[3] + t[4]) + (t[5] + t[6]))
+        ref = self.out.at[slot]
+        self.wide = [self.send(ref, ref, 2, k, dev) for k, dev in enumerate(self.devs)]
+        self.cores.append(self.send(ref, ref, 3, 7, self.c_dev))
+
+    def forward(self):
+        for k in range(7):
+            self.wide[k].wait_recv()
+            ref = self.out.at[self.c * 8 + (self.me + 7 - k) % 8]
+            self.cores.append(self.send(ref, ref, 3, k, self.c_dev))
+
+    def finish(self):
+        for d in self.cores:
+            d.wait_recv()
+
+
+def sum_scratch(rows):
     sem = pltpu.SemaphoreType.DMA
-    return pl.pallas_call(
-        gram_kernel,
-        name="gram%d" % cid,
-        out_shape=jax.ShapeDtypeStruct((16, 88, 128), F32),
-        in_specs=[VMEM],
-        out_specs=VMEM,
-        scratch_shapes=[
-            pltpu.VMEM((8, 88, 128), F32), pltpu.VMEM((8, 88, 128), F32),
-            pltpu.VMEM((7, 88, 128), F32),
-            sem, sem, sem((7,)), sem((7,)), sem((7,)), sem((7,)), sem((8,)), sem((8,)),
-        ],
-        compiler_params=params(cid),
-    )(pay)
+    return [
+        pltpu.VMEM((8, rows, 128), F32), pltpu.VMEM((8, rows, 128), F32),
+        pltpu.VMEM((7, rows, 128), F32), pltpu.VMEM((16, rows, 128), F32),
+        sem((1,)), sem((1,)), sem((7,)), sem((7,)), sem((7,)), sem((7,)), sem((8,)), sem((8,)),
+    ]
 
 
 def bl(v, k):
@@ -378,12 +387,12 @@
     )
 
 
-def unpack_gram(pay, a):
-    for n, (bi, bj) in enumerate(BLOCKS):
+def unpack_rest(pay, a):
+    for n, (bi, bj) in enumerate(BLOCKS[1:]):
         r = 128 * n
         while r < 128 * n + 128:
-            p, o = r // 80, r % 80
-            e = min(80 - o, 128 * n + 128 - r)
+            p, o = r // 72, r % 72
+            e = min(72 - o, 128 * n + 128 - r)
             q = bi * 128 + r - 128 * n
             a[q:q + e, bj * 128:(bj + 1) * 128] = pay[p, o:o + e, :]
             r += e
@@ -392,13 +401,14 @@
 def mid_kernel(parity, *refs):
     first = parity == 0
     refs = list(refs)
-    pay, sketch, theta, left, rcol, log = refs[:6]
+    pay_a, pay_b, sketch, theta, left, log = refs[:6]
     refs = refs[6:]
     if first:
         bout, lp, zs, zr, gxs, gxr, gcs, gcr = refs[:1] + refs[-7:]
         refs = refs[1:-7]
-    a, linv, part, rbc, rbd, fin = refs[:6]
-    cs, cr, ds, dr, as_, ar = refs[6:]
+    a, linv, part, rbc, rbd, fin, rcol = refs[:7]
+    cs, cr, ds, dr, as_, ar = refs[7:13]
+    scr_a, scr_b = refs[13:25], refs[25:37]
 
     s, x, y, c = place()
     is_left = s % 2 == parity
@@ -424,14 +434,23 @@
             sent.append(d)
             return d
 
-        total = jnp.sum(jnp.sum(pay[0, 80:88, :], axis=0, keepdims=True), axis=1, keepdims=True)
+        devs = [(s, bond(q // 2, q % 2, c)) for q in others]
+        sums = [
+            Sum(pay, *scr[:4], scr[4:], c, x * 2 + y, c_dev, devs, sent)
+            for pay, scr in ((pay_a, scr_a), (pay_b, scr_b))
+        ]
+        for f in ("begin", "scatter", "spread"):
+            for v in sums:
+                getattr(v, f)()
+        sums[0].forward()
+        sums[0].finish()
+        gram = scr_a[3]
+        total = jnp.sum(jnp.sum(gram[0, 8:16, :], axis=0, keepdims=True), axis=1, keepdims=True)
         mean_square = total * (1.0 / (CHI * PHYS * PHYS * CHI)) + epsilon
         log[...] = jnp.broadcast_to(0.5 * jnp.log(mean_square), (8, 128))
         scale = lax.rsqrt(mean_square) * (1.0 / root)
-        unpack_gram(pay, a)
-        ri = lax.broadcasted_iota(jnp.int32, (256, 256), 0)
-        ci = lax.broadcasted_iota(jnp.int32, (256, 256), 1)
-        perm = jnp.where(ci == (ri % 32) * 8 + ri // 32, 1.0, 0.0).astype(BF16)
+        for p in range(16):
+            a[8 * p:8 * p + 8, 0:128] = gram[p, 0:8, :]
         core, peers = {}, {}
 
         def publish(b):
@@ -439,7 +458,7 @@
             ln = (dott(sketch[:, :o + 128], linv[o:o + 128, :o + 128]) * root).astype(BF16)
             left[:, o:o + 128] = ln
             if first:
-                lp[b] = jnp.dot(perm, ln, preferred_element_type=F32).astype(BF16)
+                lp[b] = swap_rows(ln, PHYS)
                 send(lp.at[b], bout.at[b, me], zs.at[b], zr.at[b], to_left)
             lnt = ln.astype(F32).T.astype(BF16)
             for t in range(PHYS):
@@ -479,6 +498,7 @@
                 )
 
         plan = {
+            0: {8: [(lambda _: sums[1].forward(), 0)]},
             1: {9: [(step_a, 0)]},
             2: {9: [(step_a, 1)], 13: [(step_d, 0)]},
             3: {9: [(step_a, 2)], 13: [(step_d, 1)]},
@@ -500,6 +520,9 @@
             if b > 0:
                 linv[o:o + 128, :o] = -dotn(inv, t)
             publish(b)
+            if b == 0:
+                sums[1].finish()
+                unpack_rest(scr_b[3], a)
             if b < 3:
                 lb = dott(a[o + 128:, o:o + 128], inv)
                 a[o + 128:, o:o + 128] = lb
@@ -547,22 +570,26 @@
                 d.wait_send()
         for q in range(16):
             pltpu.make_async_copy(rcol.at[q], rcol.at[q], ar.at[q]).wait()
-
-
-def mid_call(pay, sketch, theta, parity, cid):
+        rows = jnp.concatenate(
+            [jnp.concatenate([rcol[2 * t], rcol[2 * t + 1]], axis=1) for t in range(PHYS)], axis=0
+        )
+        left[...] = swap_rows(rows, 32)
+
+
+def mid_call(pay_a, pay_b, sketch, theta, parity, cid):
     sem = pltpu.SemaphoreType.DMA
     first = parity == 0
     outs = [
         jax.ShapeDtypeStruct((256, CHI), BF16),
-        jax.ShapeDtypeStruct((16, 32, 256), BF16),
         jax.ShapeDtypeStruct((8, 128), F32),
     ]
     scratch = [
         pltpu.VMEM((CHI, CHI), F32), pltpu.VMEM((CHI, CHI), F32),
         pltpu.VMEM((4, 16, 128, 256), BF16), pltpu.VMEM((4, 8, 128, 256), BF16),
         pltpu.VMEM((4, 7, 128, 256), BF16), pltpu.VMEM((4, 128, 256), BF16),
+        pltpu.VMEM((16, 32, 256), BF16),
         sem((4,)), sem((4,)), sem((4, 7)), sem((4, 7)), sem((4, 4)), sem((16,)),
-    ]
+    ] + sum_scratch(16) + sum_scratch(72)
     if first:
         outs.append(jax.ShapeDtypeStruct((4, 16, 256, 128), BF16))
         scratch += [
@@ -573,40 +600,26 @@
         functools.partial(mid_kernel, parity),
         name="mid%d" % cid,
         out_shape=outs,
-        in_specs=[VMEM] * 3,
+        in_specs=[VMEM] * 4,
         out_specs=[VMEM] * len(outs),
         scratch_shapes=scratch,
         compiler_params=params(cid),
-    )(pay, sketch, theta)
-
-
-def gate_split(gates, position):
-    g = lax.dynamic_index_in_dim(gates, position, 0, keepdims=False)
-    g = g.reshape(8, 8, 8, 8).transpose(1, 0, 3, 2).reshape(64, 64)
-    hi = lax.reduce_precision(g, 8, 7)
-    lo = (g - hi).astype(BF16)
-    hi = hi.astype(BF16)
-    return jnp.concatenate([hi, hi, lo], axis=1)
+    )(pay_a, pay_b, sketch, theta)
 
 
 def shards(mps, projection, gates):
-    position = lax.axis_index("site")
-    gate3 = gate_split(gates, position)
     proj = projection[0]
-    b = gather(mps[0].transpose(1, 0, 2).reshape(256, CHI), 0)
     a = mps[0].reshape(256, CHI)
-    logs, tensors = [], []
+    b = gather(a, 0)
+    logs = []
     for parity in range(2):
-        theta, sketch, pay = theta_call(a, b, proj, gate3)
-        pay = gram_call(pay, 3 * parity + 1)
-        left, rcol, log, *more = mid_call(pay, sketch, theta, parity, 3 * parity + 2)
+        theta, sketch, pay_a, pay_b = theta_call(a, b, proj, gates)
+        a, log, *more = mid_call(pay_a, pay_b, sketch, theta, parity, parity + 1)
         b = more[0] if more else None
-        a = rcol.reshape(PHYS, 2, 32, 256).transpose(2, 0, 1, 3).reshape(256, CHI)
-        logs.append(log[0, 0:1])
-        tensors.append(left)
-    odd = position % 2 == 1
-    state = jnp.where(odd, tensors[1], a).reshape(32, PHYS, CHI)
-    return state[None], jnp.where(odd, logs[1], logs[0])
+        logs.append(log)
+    odd = lax.axis_index("site") % 2 == 1
+    log = jnp.where(odd, logs[1], logs[0])
+    return a.reshape(1, 32, PHYS, CHI), log[0, 0:1]
 
 
 def solution(mesh):

time: 228 us -> 201 us (0.88)
  Pallas kernels: 210 us -> 195 us
  local copies, waits for them, and re-layouts: 8.42 us -> 2.19 us
  between operations: 3.39 us -> 0.96 us
    pallas_call x2 -> x0, Pallas kernels: 40.9 us -> none  [gram_call(): pl.pallas_call(gram_kernel, name='gram%d' % cid, out_shape=jax.ShapeDtype...]
    pallas_call x2, Pallas kernels: 114 us -> 137 us  [mid_call(): pl.pallas_call(functools.partial(mid_kernel, parity), name='mid%d' % cid,...]
    transpose x3 -> x0, local copies, waits for them, and re-layouts: 2.96 us -> none  [the longest x1 1.73 us: shards(): b = gather(mps[0].transpose(1, 0, 2).reshape(256, CHI), 0)]
where the time goes in v2:
time: 201 us; the launch traced here: 198 us
  Pallas kernels  195 us (97%)
  local copies, waits for them, and re-layouts  2.19 us (1%)
    pallas_call x2, Pallas kernels, mid_call(): pl.pallas_call(functools.partial(mid_kernel, parity), name='mid%d' % cid,...  137 us
    pallas_call x1, Pallas kernels, gather(): pl.pallas_call(gather_kernel, name='gather%d' % cid, out_shape=jax.ShapeD...  31.7 us
    pallas_call x2, Pallas kernels, theta_call(): pl.pallas_call(theta_kernel, name='theta', out_shape=[jax.ShapeDtypeStruc...  26 us

profile of v2, /device:TPU:7, one launch (start us, length us, event | category | flops | bytes accessed | tf_op | source)
XLA Modules:
  0.0 197.8 jit_solution(10171139821298693348)
XLA Ops:
  0.6 31.7 %gather0.1.b = bf16[16,256,512]{2,1,0:T(8,128)(2,1)} custom-call(bf16[256,512]{1,0:T(8,128)(2,1)} %bitcast.6), custom_call_target="tpu_custom_call" | custom-call | tf_op jit(solution)/shard_map/gather0/pallas_call | solution.py:171
  32.4 13.0 %theta.2 = (bf16[256,4096]{1,0:T(8,128)(2,1)}, f32[256,512]{1,0:T(8,128)}, f32[16,16,128]{2,1,0:T(8,128)}, f32[16,72,128]{2,1,0:T(8,128)}) custom-call(bf16[256,512]{1,0:T(8,128)(2,1)} %bitcast.7, bf16[16,256,512]{2,1,0:T(8,128)(2,1)} %gather0.1.b, bf16[4096,512]{1,0:T(8,128)(2,1)} %bitcast.4, f32[16,64,64]{2,1,0:T(8,128)} %gates.3), custom_call_target="tpu_custom_call" | custom-call | tf_op jit(solution)/shard_map/theta/pallas_call | solution.py:262
  45.3 67.1 %mid1.1 = (bf16[256,512]{1,0:T(8,128)(2,1)}, f32[8,128]{1,0:T(8,128)}, bf16[4,16,256,128]{3,2,1,0:T(8,128)(2,1)}) custom-call(f32[16,16,128]{2,1,0:T(8,128)} %get-tuple-element.15.refs_0_, f32[16,72,128]{2,1,0:T(8,128)} %get-tuple-element.16.refs_1_, f32[256,512]{1,0:T(8,128)} %get-tuple-element.17.refs_2_, bf16[256,4096]{1,0:T(8,128)(2,1)} %get-tuple-element.18.refs_3_), custom_call_target="tpu_custom_call" | custom-call | tf_op jit(solution)/shard_map/mid1/pallas_call | solution.py:599
  112.4 0.0 copy-start
  112.5 13.0 %theta.3 = (bf16[256,4096]{1,0:T(8,128)(2,1)}, f32[256,512]{1,0:T(8,128)}, f32[16,16,128]{2,1,0:T(8,128)}, f32[16,72,128]{2,1,0:T(8,128)}) custom-call(bf16[256,512]{1,0:T(8,128)(2,1)} %get-tuple-element.19.a, bf16[4,16,256,128]{3,2,1,0:T(8,128)(2,1)} %get-tuple-element.20.b, bf16[4096,512]{1,0:T(8,128)(2,1)} %bitcast.5, f32[16,64,64]{2,1,0:T(8,128)} %gates.3), custom_call_target="tpu_custom_call" | custom-call | tf_op jit(solution)/shard_map/theta/pallas_call | solution.py:262
  125.4 69.9 %mid2.1 = (bf16[256,512]{1,0:T(8,128)(2,1)}, f32[8,128]{1,0:T(8,128)}) custom-call(f32[16,16,128]{2,1,0:T(8,128)} %get-tuple-element.21.refs_0_, f32[16,72,128]{2,1,0:T(8,128)} %get-tuple-element.22.refs_1_, f32[256,512]{1,0:T(8,128)} %get-tuple-element.23.refs_2_, bf16[256,4096]{1,0:T(8,128)(2,1)} %get-tuple-element.24.refs_3_), custom_call_target="tpu_custom_call" | custom-call | tf_op jit(solution)/shard_map/mid2/pallas_call | solution.py:599
  195.4 0.0 copy-done
  195.4 0.5 slice.3
  195.9 1.7 copy.6
  (1 shorter events, 0.0 us)
Async XLA Ops:
  112.4 82.9 %copy-start = (f32[8,128]{1,0:T(8,128)S(1)}, f32[8,128]{1,0:T(8,128)}, u32[]{:S(2)}) copy-start(f32[8,128]{1,0:T(8,128)} %get-tuple-element.27) | copy-start | bytes 12292

commit v3 on v2

--- a/solution.py
+++ b/solution.py
@@ -182,7 +182,9 @@
 BLOCKS = [(0, 0), (1, 0), (1, 1), (2, 0), (2, 1), (2, 2), (3, 0), (3, 1), (3, 2), (3, 3)]
 
 
-def theta_kernel(a, b, proj, gates, theta, sketch, pay_a, pay_b, raw):
+def theta_kernel(a, b, proj_in, gates, theta, sketch, pay_a, pay_b, raw, proj, proj_sem):
+    load = pltpu.make_async_copy(proj_in, proj, proj_sem)
+    load.start()
     a_val = a[...]
 
     def raw_step(t, _):
@@ -203,7 +205,7 @@
         raw[:, cols] = acc
         return 0
 
-    lax.fori_loop(0, PHYS, raw_step, 0)
+    lax.fori_loop(0, PHYS, raw_step, 0, unroll=2)
     gate = gates[lax.axis_index("site")]
     g_hi = gate.astype(BF16)
     g_lo = (gate - g_hi.astype(F32)).astype(BF16)
@@ -234,8 +236,9 @@
             theta[rows, v * CHI:(v + 1) * CHI] = pair.astype(BF16)
         return ss
 
-    ss = lax.fori_loop(0, 16, gate_step, jnp.zeros((8, CHI), F32))
+    ss = lax.fori_loop(0, 16, gate_step, jnp.zeros((8, CHI), F32), unroll=4)
     ss = (ss[:, 0:128] + ss[:, 128:256]) + (ss[:, 256:384] + ss[:, 384:512])
+    load.wait()
     sk = jnp.dot(theta[...], proj[...], preferred_element_type=F32)
     sketch[...] = sk
     skt = sk.T
@@ -268,9 +271,12 @@
             jax.ShapeDtypeStruct((16, 16, 128), F32),
             jax.ShapeDtypeStruct((16, 72, 128), F32),
         ],
-        in_specs=[VMEM] * 4,
+        in_specs=[VMEM, VMEM, ANY, VMEM],
         out_specs=[VMEM] * 4,
-        scratch_shapes=[pltpu.VMEM((256, PHYS * CHI), F32)],
+        scratch_shapes=[
+            pltpu.VMEM((256, PHYS * CHI), F32), pltpu.VMEM((PHYS * CHI, CHI), BF16),
+            pltpu.SemaphoreType.DMA,
+        ],
         compiler_params=params(),
     )(a, b, proj, gates)
 
@@ -406,9 +412,9 @@
     if first:
         bout, lp, zs, zr, gxs, gxr, gcs, gcr = refs[:1] + refs[-7:]
         refs = refs[1:-7]
-    a, linv, part, rbc, rbd, fin, rcol = refs[:7]
-    cs, cr, ds, dr, as_, ar = refs[7:13]
-    scr_a, scr_b = refs[13:25], refs[25:37]
+    a, linv, part, rbc, rby, rbx, rby2, rbx2, fin, rcol, lnt = refs[:11]
+    cs, cr, ds, dr, as_, ar = refs[11:17]
+    scr_a, scr_b = refs[17:29], refs[29:41]
 
     s, x, y, c = place()
     is_left = s % 2 == parity
@@ -421,7 +427,9 @@
         + [(before, q) for q in range(16)] + ([from_right] if first else []),
         25 if first else 24,
     )
-    me = c * 8 + x * 2 + y
+    me = c * 8 + y * 4 + x
+    y_dev = (s, bond(x, 1 - y, c))
+    x_devs = [(s, bond((x + k) % 4, y, c)) for k in range(1, 4)]
     root = math.sqrt(PHYS * CHI)
 
     @pl.when(is_left)
@@ -451,84 +459,130 @@
         scale = lax.rsqrt(mean_square) * (1.0 / root)
         for p in range(16):
             a[8 * p:8 * p + 8, 0:128] = gram[p, 0:8, :]
-        core, peers = {}, {}
-
-        def publish(b):
+        core, hops = {}, {}
+
+        def columns(b):
             o = b * 128
+            if b:
+                linv[o:o + 128, :o] = -dotn(
+                    linv[o:o + 128, o:o + 128], dotn(a[o:o + 128, :o], linv[:o, :o])
+                )
             ln = (dott(sketch[:, :o + 128], linv[o:o + 128, :o + 128]) * root).astype(BF16)
             left[:, o:o + 128] = ln
             if first:
                 lp[b] = swap_rows(ln, PHYS)
-                send(lp.at[b], bout.at[b, me], zs.at[b], zr.at[b], to_left)
-            lnt = ln.astype(F32).T.astype(BF16)
-            for t in range(PHYS):
-                blk = jnp.dot(
-                    lnt, theta[:, t * CHI:(t + 1) * CHI], preferred_element_type=F32
-                )
-                blk = (blk * scale).astype(BF16)
-                part[b, 2 * t] = blk[:, 0:256]
-                part[b, 2 * t + 1] = blk[:, 256:512]
+                send(lp.at[b], bout.at[b, c * 8 + x * 2 + y], zs.at[b], zr.at[b], to_left)
+            lnt[...] = ln.astype(F32).T.astype(BF16)
+
+        def partial(b, t):
+            blk = jnp.dot(
+                lnt[...], theta[:, t * CHI:(t + 1) * CHI], preferred_element_type=F32
+            )
+            blk = (blk * scale).astype(BF16)
+            part[b, 2 * t] = blk[:, 0:256]
+            part[b, 2 * t + 1] = blk[:, 256:512]
+
+        def to_core(b):
             core[b] = send(
                 part.at[b, pl.ds((1 - c) * 8, 8)], rbc.at[b], cs.at[b], cr.at[b], c_dev
             )
+
+        lo, hi = pl.ds(0, 64), pl.ds(64, 64)
+
+        def hop(b, i, src, dst, dev):
+            hops[b, i] = send(src, dst, ds.at[b, i], dr.at[b, i], dev)
 
         def step_a(b):
             core[b].wait_recv()
             half = part[b, pl.ds(c * 8, 8)].astype(F32) + rbc[b].astype(F32)
             part[b, pl.ds(c * 8, 8)] = half.astype(BF16)
-            peers[b] = [
-                send(
-                    part.at[b, c * 8 + q], rbd.at[b, k], ds.at[b, k], dr.at[b, k],
-                    (s, bond(q // 2, q % 2, c)),
-                )
-                for k, q in enumerate(others)
-            ]
+            hop(b, 0, part.at[b, pl.ds(c * 8 + (1 - y) * 4, 4), lo], rby.at[b], y_dev)
+            for k in range(3):
+                xx = (x + k + 1) % 4
+                for yy in range(2):
+                    hop(b, 1 + 2 * k + yy, part.at[b, c * 8 + yy * 4 + xx, hi],
+                        rbx.at[b, k, yy], x_devs[k])
+
+        def step_b(b):
+            hops[b, 0].wait_recv()
+            row = pl.ds(c * 8 + y * 4, 4)
+            part[b, row, lo] = (part[b, row, lo].astype(F32) + rby[b].astype(F32)).astype(BF16)
+            for k in range(3):
+                hop(b, 7 + k, part.at[b, c * 8 + y * 4 + (x + k + 1) % 4, lo],
+                    rbx2.at[b, k], x_devs[k])
+            for i in range(1, 7):
+                hops[b, i].wait_recv()
+            for yy in range(2):
+                i = c * 8 + yy * 4 + x
+                tot = (part[b, i, hi].astype(F32) + rbx[b, 0, yy].astype(F32)) + (
+                    rbx[b, 1, yy].astype(F32) + rbx[b, 2, yy].astype(F32))
+                part[b, i, hi] = tot.astype(BF16)
+            hop(b, 10, part.at[b, c * 8 + (1 - y) * 4 + x, hi], rby2.at[b], y_dev)
 
         def step_d(b):
-            for d in peers[b]:
-                d.wait_recv()
-            t = [rbd[b, k].astype(F32) for k in range(7)]
-            tot = ((part[b, me].astype(F32) + t[0]) + (t[1] + t[2])) + (
-                (t[3] + t[4]) + (t[5] + t[6]))
-            fin[b] = tot.astype(BF16)
+            for i in range(7, 11):
+                hops[b, i].wait_recv()
+            tot = (part[b, me, lo].astype(F32) + rbx2[b, 0].astype(F32)) + (
+                rbx2[b, 1].astype(F32) + rbx2[b, 2].astype(F32))
+            fin[b, lo] = tot.astype(BF16)
+            fin[b, hi] = (part[b, me, hi].astype(F32) + rby2[b].astype(F32)).astype(BF16)
             for i in range(4):
                 send(
                     fin.at[b, pl.ds(32 * i, 32)], rcol.at[me], as_.at[b, i], ar.at[me],
                     (right, 4 * b + i),
                 )
 
-        plan = {
-            0: {8: [(lambda _: sums[1].forward(), 0)]},
-            1: {9: [(step_a, 0)]},
-            2: {9: [(step_a, 1)], 13: [(step_d, 0)]},
-            3: {9: [(step_a, 2)], 13: [(step_d, 1)]},
-        }
+        def update(b):
+            o = b * 128
+            if b < 2:
+                rest = slice(o + 256, CHI)
+                lb = dott(a[rest, o:o + 128], linv[o:o + 128, o:o + 128])
+                a[rest, o:o + 128] = lb
+                a[rest, o + 128:o + 256] = a[rest, o + 128:o + 256] - dott(
+                    lb, a[o + 128:o + 256, o:o + 128])
+                a[rest, rest] = a[rest, rest] - dott(lb, lb)
+
+        plan = {0: {8: [lambda: sums[1].forward()]}}
+        for b in range(1, 4):
+            steps = {0: [functools.partial(columns, b - 1)]}
+            for t in range(PHYS):
+                steps.setdefault(1 + t // 2, []).append(functools.partial(partial, b - 1, t))
+            steps[5] = [functools.partial(to_core, b - 1)]
+            steps[6] = [functools.partial(update, b - 1)]
+            steps[13] = [functools.partial(step_a, b - 1)]
+            if b > 1:
+                steps[9] = [functools.partial(step_b, b - 2)]
+            if b > 2:
+                steps[7] = [functools.partial(step_d, b - 3)]
+            plan[b] = steps
         for b in range(4):
             o = b * 128
-            t = dotn(a[o:o + 128, :o], linv[:o, :o]) if b else None
 
             def hook(p, b=b):
-                for f, arg in plan.get(b, {}).get(p, ()):
-                    f(arg)
-
-            inv = jnp.concatenate(
+                for f in plan[b].get(p, ()):
+                    f()
+
+            linv[o:o + 128, o:o + 128] = jnp.concatenate(
                 leaf([a[o + 8 * q:o + 8 * q + 8, o:o + 128] for q in range(16)], hook), 0
             )
-            linv[o:o + 128, o:o + 128] = inv
-            if b < 3:
-                linv[o:o + 128, o + 128:] = jnp.zeros((128, CHI - o - 128), F32)
-            if b > 0:
-                linv[o:o + 128, :o] = -dotn(inv, t)
-            publish(b)
             if b == 0:
                 sums[1].finish()
                 unpack_rest(scr_b[3], a)
             if b < 3:
-                lb = dott(a[o + 128:, o:o + 128], inv)
-                a[o + 128:, o:o + 128] = lb
-                a[o + 128:, o + 128:] = a[o + 128:, o + 128:] - dott(lb, lb)
+                linv[o:o + 128, o + 128:] = jnp.zeros((128, CHI - o - 128), F32)
+                after = slice(o + 128, o + 256)
+                lb = dott(a[after, o:o + 128], linv[o:o + 128, o:o + 128])
+                a[after, o:o + 128] = lb
+                a[after, after] = a[after, after] - dott(lb, lb)
+        columns(3)
+        for t in range(PHYS):
+            partial(3, t)
+        to_core(3)
+        step_d(1)
+        step_b(2)
         step_a(3)
         step_d(2)
+        step_b(3)
         step_d(3)
         for d in sent:
             d.wait_send()
@@ -539,31 +593,68 @@
             seam = (s % 8) // 7
             sent, cores = [], []
 
-            def slot(b, q):
-                return bout.at[b, c * 8 + (q // 2) * 2 + (q % 2 + seam) % 2]
-
-            def send(ref, ss, rs, dev):
-                d = rcopy(ref, ref, ss, rs, dev)
+            def slot(b, k, other):
+                yy = (y + other + seam) % 2
+                return bout.at[b, c * 8 + ((x + 4 - k) % 4) * 2 + yy]
+
+            def send(b, i, ref, dev):
+                d = rcopy(ref, ref, gxs.at[b, i], gxr.at[b, i], dev)
                 d.start()
                 sent.append(d)
-                return d
+
+            def to_sibling(b, i, ref):
+                d = rcopy(ref, ref, gcs.at[b, i], gcr.at[b, i], c_dev)
+                d.start()
+                sent.append(d)
+                cores.append(d)
 
             def here(ref, rs):
                 pltpu.make_async_copy(ref, ref, rs).wait()
 
-            mine = x * 2 + y
-            for b in range(5):
-                if b < 4:
-                    ref = slot(b, mine)
-                    here(ref, zr.at[b])
-                    for k, q in enumerate(others):
-                        send(ref, gxs.at[b, k], gxr.at[b, k], (s, bond(q // 2, q % 2, c)))
-                    cores.append(send(ref, gcs.at[b, 7], gcr.at[b, 7], c_dev))
-                if b > 0:
-                    for k in range(7):
-                        ref = slot(b - 1, (mine + 7 - k) % 8)
-                        here(ref, gxr.at[b - 1, k])
-                        cores.append(send(ref, gcs.at[b - 1, k], gcr.at[b - 1, k], c_dev))
+            lo, hi = pl.ds(0, 128), pl.ds(128, 128)
+
+            def one(b):
+                ref = slot(b, 0, 0)
+                here(ref, zr.at[b])
+                send(b, 0, ref.at[lo], y_dev)
+                for k in range(3):
+                    send(b, 1 + k, ref.at[hi], x_devs[k])
+                for k in range(3):
+                    send(b, 4 + k, ref.at[lo], x_devs[k])
+                send(b, 13, ref.at[hi], y_dev)
+                to_sibling(b, 0, ref)
+
+            def two(b):
+                ref = slot(b, 0, 1)
+                here(ref.at[lo], gxr.at[b, 0])
+                for k in range(3):
+                    send(b, 7 + k, ref.at[lo], x_devs[k])
+                for k in range(3):
+                    ref = slot(b, k + 1, 0)
+                    here(ref.at[hi], gxr.at[b, 1 + k])
+                    send(b, 10 + k, ref.at[hi], y_dev)
+
+            def three(b):
+                for k in range(3):
+                    ref = slot(b, k + 1, 0)
+                    here(ref.at[lo], gxr.at[b, 4 + k])
+                    to_sibling(b, 1 + k, ref)
+                ref = slot(b, 0, 1)
+                here(ref.at[hi], gxr.at[b, 13])
+                to_sibling(b, 4, ref)
+                for k in range(3):
+                    ref = slot(b, k + 1, 1)
+                    here(ref.at[lo], gxr.at[b, 7 + k])
+                    here(ref.at[hi], gxr.at[b, 10 + k])
+                    to_sibling(b, 5 + k, ref)
+
+            one(0)
+            two(0)
+            for b in range(1, 4):
+                one(b)
+                three(b - 1)
+                two(b)
+            three(3)
             for d in cores:
                 d.wait_recv()
             for d in sent:
@@ -586,15 +677,17 @@
     scratch = [
         pltpu.VMEM((CHI, CHI), F32), pltpu.VMEM((CHI, CHI), F32),
         pltpu.VMEM((4, 16, 128, 256), BF16), pltpu.VMEM((4, 8, 128, 256), BF16),
-        pltpu.VMEM((4, 7, 128, 256), BF16), pltpu.VMEM((4, 128, 256), BF16),
-        pltpu.VMEM((16, 32, 256), BF16),
-        sem((4,)), sem((4,)), sem((4, 7)), sem((4, 7)), sem((4, 4)), sem((16,)),
+        pltpu.VMEM((4, 4, 64, 256), BF16), pltpu.VMEM((4, 3, 2, 64, 256), BF16),
+        pltpu.VMEM((4, 64, 256), BF16), pltpu.VMEM((4, 3, 64, 256), BF16),
+        pltpu.VMEM((4, 128, 256), BF16),
+        pltpu.VMEM((16, 32, 256), BF16), pltpu.VMEM((128, 256), BF16),
+        sem((4,)), sem((4,)), sem((4, 11)), sem((4, 11)), sem((4, 4)), sem((16,)),
     ] + sum_scratch(16) + sum_scratch(72)
     if first:
         outs.append(jax.ShapeDtypeStruct((4, 16, 256, 128), BF16))
         scratch += [
             pltpu.VMEM((4, 256, 128), BF16), sem((4,)), sem((4,)),
-            sem((4, 7)), sem((4, 7)), sem((4, 8)), sem((4, 8)),
+            sem((4, 14)), sem((4, 14)), sem((4, 8)), sem((4, 8)),
         ]
     return pl.pallas_call(
         functools.partial(mid_kernel, parity),

time: 201 us -> 193 us (0.960)
  Pallas kernels: 195 us -> 186 us
    pallas_call x2, Pallas kernels: 26 us -> 19.4 us  [theta_call(): pl.pallas_call(theta_kernel, name='theta', out_shape=[jax.ShapeDtypeStruc...]
    pallas_call x2, Pallas kernels: 137 us -> 135 us  [mid_call(): pl.pallas_call(functools.partial(mid_kernel, parity), name='mid%d' % cid,...]
where the time goes in v3:
time: 193 us; the launch traced here: 189 us
  Pallas kernels  186 us (96%)
  local copies, waits for them, and re-layouts  2.19 us (1%)
    pallas_call x2, Pallas kernels, mid_call(): pl.pallas_call(functools.partial(mid_kernel, parity), name='mid%d' % cid,...  135 us
    pallas_call x1, Pallas kernels, gather(): pl.pallas_call(gather_kernel, name='gather%d' % cid, out_shape=jax.ShapeD...  31.7 us
    pallas_call x2, Pallas kernels, theta_call(): pl.pallas_call(theta_kernel, name='theta', out_shape=[jax.ShapeDtypeStruc...  19.4 us

profile of v3, /device:TPU:7, one launch (start us, length us, event | category | flops | bytes accessed | tf_op | source)
XLA Modules:
  0.0 188.9 jit_solution(4651536924947027031)
XLA Ops:
  0.6 31.7 %gather0.1.b = bf16[16,256,512]{2,1,0:T(8,128)(2,1)} custom-call(bf16[256,512]{1,0:T(8,128)(2,1)} %bitcast.6), custom_call_target="tpu_custom_call" | custom-call | tf_op jit(solution)/shard_map/gather0/pallas_call | solution.py:171
  32.4 9.7 %theta.2 = (bf16[256,4096]{1,0:T(8,128)(2,1)}, f32[256,512]{1,0:T(8,128)}, f32[16,16,128]{2,1,0:T(8,128)}, f32[16,72,128]{2,1,0:T(8,128)}) custom-call(bf16[256,512]{1,0:T(8,128)(2,1)} %bitcast.7, bf16[16,256,512]{2,1,0:T(8,128)(2,1)} %gather0.1.b, bf16[4096,512]{1,0:T(8,128)(2,1)} %bitcast.4, f32[16,64,64]{2,1,0:T(8,128)} %gates.3), custom_call_target="tpu_custom_call" | custom-call | tf_op jit(solution)/shard_map/theta/pallas_call | solution.py:265
  42.1 65.8 %mid1.1 = (bf16[256,512]{1,0:T(8,128)(2,1)}, f32[8,128]{1,0:T(8,128)}, bf16[4,16,256,128]{3,2,1,0:T(8,128)(2,1)}) custom-call(f32[16,16,128]{2,1,0:T(8,128)} %get-tuple-element.15.refs_0_, f32[16,72,128]{2,1,0:T(8,128)} %get-tuple-element.16.refs_1_, f32[256,512]{1,0:T(8,128)} %get-tuple-element.17.refs_2_, bf16[256,4096]{1,0:T(8,128)(2,1)} %get-tuple-element.18.refs_3_), custom_call_target="tpu_custom_call" | custom-call | tf_op jit(solution)/shard_map/mid1/pallas_call | solution.py:692
  107.9 0.0 copy-start
  107.9 9.7 %theta.3 = (bf16[256,4096]{1,0:T(8,128)(2,1)}, f32[256,512]{1,0:T(8,128)}, f32[16,16,128]{2,1,0:T(8,128)}, f32[16,72,128]{2,1,0:T(8,128)}) custom-call(bf16[256,512]{1,0:T(8,128)(2,1)} %get-tuple-element.19.a, bf16[4,16,256,128]{3,2,1,0:T(8,128)(2,1)} %get-tuple-element.20.b, bf16[4096,512]{1,0:T(8,128)(2,1)} %bitcast.5, f32[16,64,64]{2,1,0:T(8,128)} %gates.3), custom_call_target="tpu_custom_call" | custom-call | tf_op jit(solution)/shard_map/theta/pallas_call | solution.py:265
  117.6 68.9 %mid2.1 = (bf16[256,512]{1,0:T(8,128)(2,1)}, f32[8,128]{1,0:T(8,128)}) custom-call(f32[16,16,128]{2,1,0:T(8,128)} %get-tuple-element.21.refs_0_, f32[16,72,128]{2,1,0:T(8,128)} %get-tuple-element.22.refs_1_, f32[256,512]{1,0:T(8,128)} %get-tuple-element.23.refs_2_, bf16[256,4096]{1,0:T(8,128)(2,1)} %get-tuple-element.24.refs_3_), custom_call_target="tpu_custom_call" | custom-call | tf_op jit(solution)/shard_map/mid2/pallas_call | solution.py:692
  186.5 0.0 copy-done
  186.5 0.5 slice.3
  187.0 1.7 copy.6
  (1 shorter events, 0.0 us)
Async XLA Ops:
  107.9 78.6 %copy-start = (f32[8,128]{1,0:T(8,128)S(1)}, f32[8,128]{1,0:T(8,128)}, u32[]{:S(2)}) copy-start(f32[8,128]{1,0:T(8,128)} %get-tuple-element.27) | copy-start | bytes 12292
